TPU v7x, 32 devices: a whole 2x2x4 slice. The times are simulated.
32 devices in a mesh: grp: 16 (over z, y, x), tp: 2 (over core).
Axes of the slice: x: 2, y: 2, z: 4, core: 2. Of those that a mesh axis runs over, the one named last changes fastest.
Arguments:
- normed_token_input: bfloat16 [16384, 4096], P('grp', 'tp'), may hold values from -6 to 6
- queries: bfloat16 [16384, 4096], P('grp', 'tp'), may hold values from -6 to 6
- fresh_token_keys: bfloat16 [16384, 1024], P('grp', 'tp'), may hold values from -6 to 6
- fresh_token_values: bfloat16 [16384, 1024], P('grp', 'tp'), may hold values from -6 to 6
- token_request_index: int32 [16384], P('grp'), may hold values from 0 to 63, never falling along the last dimension, each value on 1 to 1024 neighbouring positions
- prefix_page_cache: bfloat16 [32, 2, 128, 1024], P('grp', None, None, 'tp'), may hold values from -6 to 6
- adapter_down_weight: bfloat16 [32, 16, 4096], P('grp', None, 'tp'), may hold values from -0.09375 to 0.09375
- adapter_up_weight: bfloat16 [32, 16, 4096], P('grp', None, 'tp'), may hold values from -1.5 to 1.5
- group_page_list: int32 [16, 4], replicated, may hold values from 0 to 31, as said below
- group_adapter_list: int32 [16, 4], replicated, may hold values from 0 to 31, as said below
- page_entry_index: int32 [64], replicated, may hold values from 0 to 3
- adapter_entry_index: int32 [64], replicated, may hold values from 0 to 3
Outputs:
- attended: bfloat16 [16384, 4096], P('grp', 'tp')
Inputs may be any that keep to these rules, and one draw needn't show every extreme that they name: `group_page_list`: the 4 pages of a row lie with distinct owners: page // 2 differs within a row. `group_adapter_list`: the 4 adapters of a row lie with distinct owners: adapter // 2 differs within a row.
All inputs are finite; a program needn't handle non-finite values.
Results may differ from a plain program's by a relative error of at most 0.0065.
Values may be sent and summed in bfloat16 or wider, within the bound.
No kernel may reach another device: no remote copies, remote signals or barrier semaphores. Data moves between devices by JAX's collectives and lax.ppermute only.
A program may use at most 64 MiB of HBM per device.

v0:
```python
import jax
import jax.numpy as jnp
from jax import lax
from jax.sharding import PartitionSpec as P

QUERY_HEADS = 32
KV_HEADS = 8
HEAD_WIDTH = 128
PAGE = 128


adapter_scale = 0.5


def passed_along(shard, axis, by):
    peers = lax.axis_size(axis)
    pairs = [(i, i + by) for i in range(peers) if 0 <= i + by < peers]
    return lax.ppermute(shard, axis, pairs)


def local(
    normed_token_input,
    queries,
    fresh_token_keys,
    fresh_token_values,
    token_request_index,
    prefix_page_cache,
    adapter_down_weight,
    adapter_up_weight,
    group_page_list,
    group_adapter_list,
    page_entry_index,
    adapter_entry_index,
):
    groups = lax.axis_size("grp")
    own_group = lax.axis_index("grp")
    tokens = queries.shape[0]
    adapters_used = group_adapter_list.shape[1]
    rank_width = adapter_down_weight.shape[1]
    key_width = fresh_token_keys.shape[1]
    head_dim = HEAD_WIDTH
    kv_local = key_width // head_dim
    heads_local = queries.shape[1] // head_dim
    per_kv = QUERY_HEADS // KV_HEADS
    group_pick = (jnp.arange(groups, dtype=jnp.int32) == own_group).astype(jnp.int32)
    page_row = jnp.sum(group_pick[:, None] * group_page_list, axis=0)
    adapter_entry_row = jnp.sum(group_pick[:, None] * group_adapter_list, axis=0)
    pieces = (
        lax.all_gather(prefix_page_cache, "grp", axis=0, tiled=True),
        lax.all_gather(adapter_down_weight, "grp", axis=0, tiled=True),
        lax.all_gather(adapter_up_weight, "grp", axis=0, tiled=True),
    )
    count = pieces[0].shape[0]
    stored = jnp.arange(count, dtype=jnp.int32)
    page_pick = (page_row[:, None] == stored[None, :]).astype(jnp.bfloat16)
    adapter_pick = (adapter_entry_row[:, None] == stored[None, :]).astype(jnp.bfloat16)
    pages = jnp.einsum(
        "pn,nabc->pabc", page_pick, pieces[0], preferred_element_type=jnp.float32
    ).astype(jnp.bfloat16)
    down_factors = jnp.einsum(
        "pn,nrd->prd", adapter_pick, pieces[1], preferred_element_type=jnp.float32
    ).astype(jnp.bfloat16)
    up_factors = jnp.einsum(
        "pn,nrd->prd", adapter_pick, pieces[2], preferred_element_type=jnp.float32
    ).astype(jnp.bfloat16)
    requests = jnp.arange(page_entry_index.shape[0], dtype=jnp.int32)
    member = (token_request_index[:, None] == requests[None, :]).astype(jnp.int32)
    page_of = jnp.sum(member * page_entry_index[None, :], axis=1)
    adapter_of = jnp.sum(member * adapter_entry_index[None, :], axis=1)
    adapter_mask = (
        adapter_of[:, None] == jnp.arange(adapters_used, dtype=jnp.int32)[None, :]
    ).astype(jnp.float32)
    expanded = jnp.repeat(adapter_mask, rank_width, axis=1)
    partial_terms = (
        jnp.einsum(
            "td,kd->tk",
            normed_token_input,
            down_factors.reshape(adapters_used * rank_width, -1),
            preferred_element_type=jnp.float32,
        )
        * expanded
    )
    summed = lax.psum(partial_terms, "tp")
    lowrank = summed.astype(jnp.bfloat16)
    query_update = jnp.dot(
        lowrank,
        up_factors.reshape(adapters_used * rank_width, -1),
        preferred_element_type=jnp.float32,
    )
    query_adapted = (queries.astype(jnp.float32) + adapter_scale * query_update).astype(
        jnp.bfloat16
    )
    stacked = jnp.stack([fresh_token_keys, fresh_token_values])
    before = passed_along(stacked, "grp", 1)
    before_ids = passed_along(token_request_index + 1, "grp", 1)
    page_keys = pages[:, 0].reshape(-1, key_width)
    page_values = pages[:, 1].reshape(-1, key_width)
    keys_all = (
        jnp.concatenate([page_keys, before[0], fresh_token_keys], 0)
        .reshape(-1, kv_local, head_dim)
        .transpose(1, 0, 2)
    )
    values_all = (
        jnp.concatenate([page_values, before[1], fresh_token_values], 0)
        .reshape(-1, kv_local, head_dim)
        .transpose(1, 0, 2)
    )
    page_cols = jnp.arange(page_keys.shape[0], dtype=jnp.int32) // PAGE
    see_page = page_of[:, None] == page_cols[None, :]
    see_prev = before_ids[None, :] == token_request_index[:, None] + 1
    order = jnp.arange(tokens, dtype=jnp.int32)
    see_own = (token_request_index[None, :] == token_request_index[:, None]) & (
        order[None, :] <= order[:, None]
    )
    visible = jnp.concatenate([see_page, see_prev, see_own], 1)
    block = min(512, tokens)
    nblocks = tokens // block
    query_three = query_adapted.reshape(tokens, heads_local, head_dim)

    def one_block(counter):
        head = counter // nblocks
        first_row = counter % nblocks * block
        rows = lax.dynamic_slice_in_dim(query_three, first_row, block, 0)
        query_head = lax.dynamic_index_in_dim(rows, head, 1, keepdims=False)
        key_head = lax.dynamic_index_in_dim(keys_all, head // per_kv, 0, keepdims=False)
        value_head = lax.dynamic_index_in_dim(values_all, head // per_kv, 0, keepdims=False)
        sight = lax.dynamic_slice_in_dim(visible, first_row, block, 0)
        scores = jnp.einsum("qd,kd->qk", query_head, key_head, preferred_element_type=jnp.float32)
        scores = jnp.where(sight, scores * HEAD_WIDTH ** (-0.5), jnp.float32(-1e30))
        highest = jnp.max(scores, axis=1, keepdims=True)
        expo = jnp.where(sight, jnp.exp(scores - highest), jnp.float32(0.0))
        weights = (expo / jnp.sum(expo, axis=1, keepdims=True)).astype(jnp.bfloat16)
        return jnp.dot(weights, value_head, preferred_element_type=jnp.float32).astype(jnp.bfloat16)

    outputs = lax.map(one_block, jnp.arange(heads_local * nblocks, dtype=jnp.int32))
    return (
        outputs.reshape(heads_local, tokens, head_dim)
        .transpose(1, 0, 2)
        .reshape(tokens, heads_local * head_dim)
    )


def solution(mesh):
    placed = (
        P("grp", "tp"),
        P("grp", "tp"),
        P("grp", "tp"),
        P("grp", "tp"),
        P("grp"),
        P("grp", None, None, "tp"),
        P("grp", None, "tp"),
        P("grp", None, "tp"),
        P(),
        P(),
        P(),
        P(),
    )
    return jax.shard_map(
        local, mesh=mesh, in_specs=placed, out_specs=P("grp", "tp"), check_vma=False
    )
```

profile of v0, /device:TPU:16, one launch (start us, length us, event | category | flops | bytes accessed | tf_op | source)
XLA Modules:
  0.0 621.2 jit_solution(2944425719761467936)
XLA Ops:
  13.8 3.4 collective-permute-start.1
  17.3 3.4 collective-permute-start
  23.0 62.0 %collective-permute-done = s32[1024]{0:T(1024)S(1)} collective-permute-done((s32[1024]{0:T(1024)S(1)}, s32[1024]{0:T(1024)S(1)}, u32[]{:S(2)}, u32[]{:S(2)}) %collective-permute-start) | collective-permute-done | bytes 4128 | tf_op jit(solution)/shard_map/ppermute | solution.py:18
  85.7 3.3 pad_add_fusion
  89.0 3.0 fusion.38
  92.0 3.9 convolution_convert_fusion.1
  96.1 3.6 fusion.23
  99.7 46.9 %all-gather.6.cloned.1.call-done = bf16[32,16,2048]{2,1,0:T(8,128)(2,1)} async-done(((bf16[2,16,2048]{2,1,0:T(8,128)(2,1)}), bf16[32,16,2048]{2,1,0:T(8,128)(2,1)}) %all-gather.6.cloned.1.call-update) | async-done | bytes 2097168 | tf_op jit(solution)/shard_map/all_gather | solution.py:51
  146.6 3.9 convolution_convert_fusion
  150.7 4.3 all-reduce.1
  155.1 3.6 fusion.17
  158.7 3.0 copy.88
  161.7 99.0 %all-gather.8.cloned.1.call-done = bf16[32,2,128,512]{3,2,1,0:T(8,128)(2,1)} async-done(((bf16[2,2,128,512]{3,2,1,0:T(8,128)(2,1)}), bf16[32,2,128,512]{3,2,1,0:T(8,128)(2,1)}) %all-gather.8.cloned.1.call-update) | async-done | bytes 8388624 | tf_op jit(solution)/shard_map/all_gather | solution.py:49
  260.7 8.2 %fusion.20 = bf16[4,2,128,512]{3,0,2,1:T(4,128)(2,1)S(1)} fusion(bf16[32,2,128,512]{3,2,1,0:T(8,128)(2,1)} %all-gather.8.cloned.1.call-done, s32[4]{0:T(128)S(1)} %get-tuple-element.156), kind=kOutput, calls=%fused_computation.34 | convolution fusion | flops 34078848 | bytes 9437200 | tf_op jit(solution)/shard_map/pn,nabc->pabc/dot_general | solution.py:57
  276.8 4.1 maximum_bitcast_fusion
  280.9 324.7 %while.13 = (s32[]{:T(128)}, bf16[32,512,128]{2,1,0:T(8,128)(2,1)}, s32[32]{0:T(128)S(1)}, pred[1024,2560]{1,0:T(32,128)(4,1)S(1)}, bf16[1024,16,128]{2,0,1:T(8,...) while((s32[]{:T(128)}, bf16[32,512,128]{2,1,0:T(8,128)(2,1)}, ...), condition=%wide.region_8.9_spmd, body=%wide.region_5.8_spmd.sunk | while | flops 684260352 | bytes 21245088 | solution.py:135
  284.0 2.5 fusion.49
  287.8 3.2 fusion.51
  298.0 3.2 fusion.51
  304.3 2.4 fusion.49
  308.1 3.2 fusion.51
  318.3 3.2 fusion.51
  324.6 2.4 fusion.49
  328.4 3.2 fusion.51
  338.6 3.2 fusion.51
  344.9 2.4 fusion.49
  348.7 3.2 fusion.51
  358.9 3.2 fusion.51
  365.2 2.4 fusion.49
  369.0 3.2 fusion.51
  379.2 3.2 fusion.51
  385.5 2.4 fusion.49
  389.3 3.2 fusion.51
  399.5 3.2 fusion.51
  405.8 2.4 fusion.49
  409.6 3.2 fusion.51
  419.7 3.2 fusion.51
  426.1 2.4 fusion.49
  429.9 3.2 fusion.51
  440.0 3.2 fusion.51
  446.4 2.4 fusion.49
  450.2 3.2 fusion.51
  460.3 3.2 fusion.51
  466.7 2.4 fusion.49
  470.5 3.2 fusion.51
  480.6 3.2 fusion.51
  487.0 2.4 fusion.49
  490.8 3.2 fusion.51
  500.9 3.2 fusion.51
  507.3 2.4 fusion.49
  511.1 3.2 fusion.51
  521.2 3.2 fusion.51
  531.4 3.2 fusion.51
  541.5 3.2 fusion.51
  551.7 3.2 fusion.51
  561.8 3.2 fusion.51
  568.2 2.4 fusion.49
  572.0 3.2 fusion.51
  582.1 3.2 fusion.51
  588.5 2.4 fusion.49
  592.3 3.2 fusion.51
  602.4 3.2 fusion.51
  605.6 4.9 copy.67
  610.5 4.1 copy.87
  (126 shorter events, 123.9 us)
Async XLA Ops:
  6.5 85.5 %all-gather.4.cloned.1.call-start = ((), (), s32[]{:S(2)}) async-start(), calls=%async_computation | async-start | bytes 2228224 | tf_op jit(solution)/shard_map/all_gather | solution.py:50
  7.3 139.4 %all-gather.6.cloned.1.call-start = ((), (), s32[]{:S(2)}) async-start(), calls=%async_computation.1 | async-start | bytes 2228224 | tf_op jit(solution)/shard_map/all_gather | solution.py:51
  8.0 252.7 %all-gather.8.cloned.1.call-start = ((), (), s32[]{:S(2)}) async-start(), calls=%async_computation.2 | async-start | bytes 8912896 | tf_op jit(solution)/shard_map/all_gather | solution.py:49
  8.7 8.5 %copy-start.2 = (s32[1024]{0:T(1024)S(1)}, s32[1024]{0:T(1024)}, u32[]{:S(2)}) copy-start(s32[1024]{0:T(1024)} %param.18) | copy-start | bytes 12292
  8.8 11.9 %copy-start.5 = (s32[64]{0:T(128)S(1)}, s32[64]{0:T(128)}, u32[]{:S(2)}) copy-start(s32[64]{0:T(128)} %param.25) | copy-start | bytes 772
  8.8 11.9 %copy-start.6 = (s32[64]{0:T(128)S(1)}, s32[64]{0:T(128)}, u32[]{:S(2)}) copy-start(s32[64]{0:T(128)} %param.24) | copy-start | bytes 772
  10.3 74.7 %copy-start = (bf16[1024,512]{0,1:T(8,128)(2,1)}, bf16[1024,512]{0,1:T(8,128)(2,1)S(1)}, u32[]{:S(2)}) copy-start(bf16[1024,512]{0,1:T(8,128)(2,1)S(1)} %copy.57) | copy-start | bytes 3145732
  10.3 12.5 %copy-start.3 = (s32[16,4]{0,1:T(4,128)S(1)}, s32[16,4]{0,1:T(4,128)}, u32[]{:S(2)}) copy-start(s32[16,4]{0,1:T(4,128)} %param.22) | copy-start | bytes 772
  10.3 12.5 %copy-start.4 = (s32[16,4]{0,1:T(4,128)S(1)}, s32[16,4]{0,1:T(4,128)}, u32[]{:S(2)}) copy-start(s32[16,4]{0,1:T(4,128)} %param.23) | copy-start | bytes 772
  12.2 72.8 %copy-start.1 = (bf16[1024,512]{0,1:T(8,128)(2,1)}, bf16[1024,512]{0,1:T(8,128)(2,1)S(1)}, u32[]{:S(2)}) copy-start(bf16[1024,512]{0,1:T(8,128)(2,1)S(1)} %copy.58) | copy-start | bytes 3145732
  13.8 75.1 %collective-permute-start.1 = (bf16[2,1024,512]{1,2,0:T(8,128)(2,1)}, bf16[2,1024,512]{1,2,0:T(8,128)(2,1)}, u32[]{:S(2)}, u32[]{:S(2)}) collective-permute-start(bf16[2,1024,512]{1,2,0:T(8,128)(2,1)} %pad_maximum_fusion), channel_id=1, source_target_pairs={{0,2},{2,4},{4,6},{6,8},{8,10},{10,12},{12,14},{14,16},{16,18},{18... | collective-permute-start | bytes 6291464 | tf_op jit(solution)/shard_map/ppermute | solution.py:18
  17.3 67.7 %collective-permute-start = (s32[1024]{0:T(1024)S(1)}, s32[1024]{0:T(1024)S(1)}, u32[]{:S(2)}, u32[]{:S(2)}) collective-permute-start(s32[1024]{0:T(1024)S(1)} %broadcast_add_fusion), channel_id=1, source_target_pairs={{0,2},{2,4},{4,6},{6,8},{8,10},{10,12},{12,14},{14,16},{16,18},{18... | collective-permute-start | bytes 12296 | tf_op jit(solution)/shard_map/ppermute | solution.py:18
Sparse Core Ops, SparseCore 0:
  10.1 73.1 all-gather.3
  86.1 60.4 all-gather.5
  149.4 111.2 all-gather.7
where the time goes:
time: 628 us; the launch traced here: 621 us
  waiting for transfers between devices  210 us (33%)
  matrix products  205 us (33%)
  loops' own time  81.5 us (13%)
  other arithmetic  54.5 us (9%)
  local copies, waits for them, and re-layouts  45.7 us (7%)
  between operations  13.3 us (2%)
  starting transfers between devices  6.87 us (1%)
    dot_general x32, matrix products, one_block(): jnp.dot(weights, value_head, preferred_element_type=jnp.float32)  103 us
    all_gather x1, waiting for transfers between devices, local(): lax.all_gather(prefix_page_cache, 'grp', axis=0, tiled=True)  99 us
    another operation x1, loops' own time, local(): lax.map(one_block, jnp.arange(heads_local * nblocks, dtype=jnp.int32))  81.5 us
    dot_general x32, matrix products, one_block(): jnp.einsum('qd,kd->qk', query_head, key_head, preferred_element_type=jnp....  78.4 us
    ppermute x2, waiting for transfers between devices, passed_along(): return lax.ppermute(shard, axis, pairs)  62 us
    all_gather x1, waiting for transfers between devices, local(): lax.all_gather(adapter_up_weight, 'grp', axis=0, tiled=True)  46.9 us
    reduce_sum x32, other arithmetic, one_block(): weights = (expo / jnp.sum(expo, axis=1, keepdims=True)).astype(jnp.bfloat16)  42.5 us
    dynamic_slice x32, local copies, waits for them, and re-layouts, local(): lax.map(one_block, jnp.arange(heads_local * nblocks, dtype=jnp.int32))  19 us
  transfers between devices with their start and end apart: 5, of which 3 were waited for; matrix products, arithmetic and copies ran while one was open for 5% of the time, Pallas kernels for 0%

commit v1 on v0

v1 whole, which is shorter than its diff:
```python
import math

import jax
import jax.numpy as jnp
from jax import lax
from jax.experimental import pallas as pl
from jax.experimental.pallas import tpu as pltpu
from jax.sharding import PartitionSpec as P

QUERY_HEADS = 32
KV_HEADS = 8
HEAD_WIDTH = 128
PAGE = 128
PER_KV = QUERY_HEADS // KV_HEADS

adapter_scale = 0.5

SCORE_SCALE = HEAD_WIDTH ** (-0.5) * math.log2(math.e)
UNSEEN = -1e30

ONES_ROWS = 16
STATE_ROWS = HEAD_WIDTH + ONES_ROWS
SUM_ROW = HEAD_WIDTH
MAX_ROW = HEAD_WIDTH + 8

VMEM_LIMIT = 48 * 1024 * 1024


def columns_of(groups):
    columns = 1
    while columns * columns < groups and groups % (2 * columns) == 0:
        columns *= 2
    return columns


def gather_column(own, groups, columns):
    rows = groups // columns
    down = [(i, i + columns) for i in range(groups - columns)]
    up = [(i + columns, i) for i in range(groups - columns)]
    from_below, from_above = [], []
    lower = upper = own
    for _ in range(rows - 1):
        lower = lax.ppermute(lower, "grp", down)
        upper = lax.ppermute(upper, "grp", up)
        from_below.append(lower)
        from_above.append(upper)
    return from_below[::-1] + [own] + from_above


def pick_units(wanted, stacks, name):
    count = wanted.shape[0]
    unit = stacks[0].shape[1:]

    def body(wanted_ref, *refs):
        sources = refs[: len(stacks)]
        outputs = refs[len(stacks) : len(stacks) + count]
        sems = refs[-1]
        for m in range(count):
            for k, source in enumerate(sources):

                @pl.when(wanted_ref[m, 0] == k)
                def _():
                    pltpu.make_async_copy(
                        source.at[wanted_ref[m, 1]], outputs[m], sems.at[m]
                    ).start()

        for m in range(count):
            pltpu.make_async_copy(sources[0].at[0], outputs[m], sems.at[m]).wait()

    return pl.pallas_call(
        body,
        out_shape=[jax.ShapeDtypeStruct(unit, stacks[0].dtype)] * count,
        in_specs=[pl.BlockSpec(memory_space=pltpu.SMEM)]
        + [pl.BlockSpec(memory_space=pl.ANY)] * len(stacks),
        out_specs=[pl.BlockSpec(memory_space=pl.ANY)] * count,
        scratch_shapes=[pltpu.SemaphoreType.DMA((count,))],
        name=name,
    )(wanted, *stacks)


def deliver(own, listed, groups, columns, name):
    rows = groups // columns
    stored = own.shape[0]
    entries = listed.shape[1]
    me = lax.axis_index("grp")
    row, column = me // columns, me % columns
    stacks = gather_column(own, groups, columns)

    owner = listed // stored
    place = listed % stored
    owner_row, owner_column = owner // columns, owner % columns
    same = owner_column[:, :, None] == owner_column[:, None, :]
    earlier = jnp.arange(entries)[None, :] < jnp.arange(entries)[:, None]
    rank = jnp.sum((same & earlier[None]).astype(jnp.int32), axis=2)
    rounds = jnp.max(rank) + 1

    masks = jnp.arange(columns, dtype=jnp.int32)
    partner = row * columns + (column ^ masks)
    partner_pick = (partner[:, None] == jnp.arange(groups)[None, :]).astype(jnp.int32)

    def of_partner(table):
        return jnp.sum(partner_pick[:, :, None] * table[None], axis=1)

    his_column, his_rank = of_partner(owner_column), of_partner(rank)
    his_stack = of_partner(owner_row) - row + rows - 1
    his_place = of_partner(place)

    def exchange(turn):
        here = ((his_column == column) & (his_rank == turn)).astype(jnp.int32)
        some = jnp.sum(here, axis=1)
        stack = jnp.sum(here * his_stack, axis=1) + (1 - some) * (rows - 1)
        wanted = jnp.stack([stack, jnp.sum(here * his_place, axis=1)], axis=1)
        units = pick_units(wanted, stacks, name)
        return [units[0]] + [
            lax.ppermute(units[m], "grp", [(i, i ^ m) for i in range(groups)])
            for m in range(1, columns)
        ]

    my_mask = his_column[0] ^ column
    my_rank = his_rank[0]
    first = my_rank == 0
    used = jnp.any(first[:, None] & (my_mask[:, None] == masks[None, :]), axis=0)
    free_order = jnp.cumsum(1 - used.astype(jnp.int32)) - 1
    later_order = jnp.cumsum(1 - first.astype(jnp.int32)) - 1
    fits = (~used)[None, :] & (free_order[None, :] == later_order[:, None])
    spare = jnp.sum(fits.astype(jnp.int32) * masks[None, :], axis=1)
    buffer_of = jnp.where(first, my_mask, spare)

    buffers = exchange(jnp.int32(0))

    def another(carry):
        turn, held = carry
        held = list(held)
        arrived = exchange(turn)
        for b in range(columns):
            for m in range(columns):
                lands = jnp.any((my_rank == turn) & (my_mask == m) & (buffer_of == b))
                held[b] = jnp.where(lands, arrived[m], held[b])
        return turn + 1, tuple(held)

    _, buffers = lax.while_loop(
        lambda carry: carry[0] < rounds, another, (jnp.int32(1), tuple(buffers))
    )
    return buffers, buffer_of


def low_rank_part(normed, factors, rank_width):
    tokens, width = normed.shape
    block = min(256, tokens)
    total = rank_width * len(factors)

    def body(x_ref, *refs):
        down = jnp.concatenate([f[:rank_width, :] for f in refs[:-1]], axis=0)
        refs[-1][...] = lax.dot_general(
            x_ref[...], down, (((1,), (1,)), ((), ())), preferred_element_type=jnp.float32
        )

    return pl.pallas_call(
        body,
        grid=(tokens // block,),
        out_shape=jax.ShapeDtypeStruct((tokens, total), jnp.float32),
        in_specs=[pl.BlockSpec((block, width), lambda i: (i, 0))]
        + [pl.BlockSpec(f.shape, lambda i: (0, 0)) for f in factors],
        out_specs=pl.BlockSpec((block, total), lambda i: (i, 0)),
        compiler_params=pltpu.CompilerParams(vmem_limit_bytes=VMEM_LIMIT),
        cost_estimate=pl.CostEstimate(
            flops=2 * tokens * width * total,
            bytes_accessed=2 * tokens * width,
            transcendentals=0,
        ),
        name="low_rank_part",
    )(normed, *factors)


def absorb(scores, values_t, acc_ref, max_ref, head):
    held = max_ref[head : head + 1, :]
    highest = jnp.maximum(held, jnp.max(scores, axis=0, keepdims=True))
    weights = jnp.exp2(scores - highest).astype(jnp.bfloat16)
    fade = jnp.exp2(held - highest)
    max_ref[head : head + 1, :] = highest
    acc_ref[head] = acc_ref[head] * fade + jnp.dot(
        values_t, weights, preferred_element_type=jnp.float32
    )


def scores_of(keys, query):
    return (
        lax.dot_general(
            keys, query, (((1,), (1,)), ((), ())), preferred_element_type=jnp.float32
        )
        * SCORE_SCALE
    )


def transposed(values):
    return values.astype(jnp.float32).T.astype(jnp.bfloat16)


def fresh_attention(
    queries, low_rank, factors, rank_width, keys_before, values_before, keys, values, begin
):
    tokens, width = queries.shape
    kv_local = keys.shape[1] // HEAD_WIDTH
    heads_local = width // HEAD_WIDTH
    span = PER_KV * HEAD_WIDTH
    block = min(256, tokens)
    tile = min(256, tokens)
    blocks = tokens // block
    first_tile = begin.reshape(blocks, block)[:, 0] // tile

    def body(first_ref, q_ref, lr_ref, kb_ref, vb_ref, k_ref, v_ref, begin_ref, *refs):
        factor_refs = refs[: len(factors)]
        state_ref, adapted_ref, keys_ref, values_ref, acc_ref, max_ref = refs[len(factors) :]
        step = pl.program_id(1)

        @pl.when(step == 0)
        def _():
            keys_ref[:tokens, :] = kb_ref[...]
            keys_ref[tokens:, :] = k_ref[...]
            values_ref[:HEAD_WIDTH, :tokens] = transposed(vb_ref[...])
            values_ref[:HEAD_WIDTH, tokens:] = transposed(v_ref[...])
            values_ref[HEAD_WIDTH:, :] = jnp.ones((ONES_ROWS, 2 * tokens), jnp.bfloat16)

        up = jnp.concatenate([f[rank_width:, :] for f in factor_refs], axis=0)
        update = jnp.dot(lr_ref[...], up, preferred_element_type=jnp.float32)
        adapted_ref[...] = (
            q_ref[...].astype(jnp.float32) + adapter_scale * update
        ).astype(jnp.bfloat16)

        acc_ref[...] = jnp.zeros_like(acc_ref)
        max_ref[...] = jnp.full_like(max_ref, UNSEEN)
        start = begin_ref[...]
        own = tokens + step * block + lax.broadcasted_iota(jnp.int32, (1, block), 1)

        def one_tile(number, _):
            at = pl.multiple_of(number * tile, tile)
            key_rows = keys_ref[pl.ds(at, tile), :]
            values_t = values_ref[:, pl.ds(at, tile)]
            position = at + lax.broadcasted_iota(jnp.int32, (tile, block), 0)
            seen = (position >= start) & (position <= own)
            for head in range(PER_KV):
                query = adapted_ref[:, head * HEAD_WIDTH : (head + 1) * HEAD_WIDTH]
                scores = jnp.where(seen, scores_of(key_rows, query), UNSEEN)
                absorb(scores, values_t, acc_ref, max_ref, head)
            return 0

        last = (tokens + (step + 1) * block + tile - 1) // tile
        lax.fori_loop(first_ref[step], last, one_tile, 0)
        for head in range(PER_KV):
            state_ref[head, :MAX_ROW, :] = acc_ref[head, :MAX_ROW, :]
            state_ref[head, MAX_ROW:, :] = jnp.broadcast_to(
                max_ref[head : head + 1, :], (STATE_ROWS - MAX_ROW, block)
            )

    by_head = lambda h, i, first: (0, h)
    by_block = lambda h, i, first: (i, h)
    whole = pl.BlockSpec((tokens, HEAD_WIDTH), by_head)
    return pl.pallas_call(
        body,
        grid_spec=pltpu.PrefetchScalarGridSpec(
            num_scalar_prefetch=1,
            grid=(kv_local, blocks),
            in_specs=[
                pl.BlockSpec((block, span), by_block),
                pl.BlockSpec((block, low_rank.shape[1]), lambda h, i, first: (i, 0)),
                whole,
                whole,
                whole,
                whole,
                pl.BlockSpec((1, block), lambda h, i, first: (0, i)),
            ]
            + [pl.BlockSpec((f.shape[0], span), by_head) for f in factors],
            out_specs=[
                pl.BlockSpec((PER_KV, STATE_ROWS, block), lambda h, i, first: (h, 0, i)),
                pl.BlockSpec((block, span), by_block),
            ],
            scratch_shapes=[
                pltpu.VMEM((2 * tokens, HEAD_WIDTH), jnp.bfloat16),
                pltpu.VMEM((STATE_ROWS, 2 * tokens), jnp.bfloat16),
                pltpu.VMEM((PER_KV, STATE_ROWS, block), jnp.float32),
                pltpu.VMEM((8, block), jnp.float32),
            ],
        ),
        out_shape=[
            jax.ShapeDtypeStruct((heads_local, STATE_ROWS, tokens), jnp.float32),
            jax.ShapeDtypeStruct((tokens, width), jnp.bfloat16),
        ],
        compiler_params=pltpu.CompilerParams(vmem_limit_bytes=VMEM_LIMIT),
        cost_estimate=pl.CostEstimate(
            flops=4 * tokens * tokens * width // 2,
            bytes_accessed=20 * 1024 * 1024,
            transcendentals=heads_local * tokens * tokens // 2,
        ),
        name="fresh_attention",
    )(
        first_tile,
        queries,
        low_rank,
        keys_before,
        values_before,
        keys,
        values,
        begin.reshape(1, tokens),
        *factors,
    )


def page_attention(state, adapted, buffers, page_buffer):
    tokens, width = adapted.shape
    span = PER_KV * HEAD_WIDTH
    kv_local = width // span
    block = min(256, tokens)
    blocks = tokens // block
    count = len(buffers)
    uses = jnp.any(
        page_buffer.reshape(blocks, block, 1) == jnp.arange(count)[None, None, :], axis=1
    ).astype(jnp.int32)

    def body(uses_ref, state_ref, q_ref, which_ref, *refs):
        page_refs = refs[:count]
        out_ref, values_ref, acc_ref, max_ref = refs[count:]
        step = pl.program_id(1)

        @pl.when(step == 0)
        def _():
            for b in range(count):
                values_ref[b, :HEAD_WIDTH, :] = transposed(page_refs[b][PAGE:, :])
                values_ref[b, HEAD_WIDTH:, :] = jnp.ones((ONES_ROWS, PAGE), jnp.bfloat16)

        for head in range(PER_KV):
            acc_ref[head] = state_ref[head]
            max_ref[head : head + 1, :] = state_ref[head, MAX_ROW : MAX_ROW + 1, :]
        which = which_ref[...]
        for b in range(count):

            @pl.when(uses_ref[step, b] != 0)
            def _():
                seen = which == b
                for head in range(PER_KV):
                    query = q_ref[:, head * HEAD_WIDTH : (head + 1) * HEAD_WIDTH]
                    scores = jnp.where(seen, scores_of(page_refs[b][:PAGE, :], query), UNSEEN)
                    absorb(scores, values_ref[b], acc_ref, max_ref, head)

        for head in range(PER_KV):
            result = acc_ref[head, :HEAD_WIDTH, :] / acc_ref[head, SUM_ROW : SUM_ROW + 1, :]
            out_ref[:, head * HEAD_WIDTH : (head + 1) * HEAD_WIDTH] = result.T.astype(
                jnp.bfloat16
            )

    return pl.pallas_call(
        body,
        grid_spec=pltpu.PrefetchScalarGridSpec(
            num_scalar_prefetch=1,
            grid=(kv_local, blocks),
            in_specs=[
                pl.BlockSpec((PER_KV, STATE_ROWS, block), lambda h, i, uses: (h, 0, i)),
                pl.BlockSpec((block, span), lambda h, i, uses: (i, h)),
                pl.BlockSpec((1, block), lambda h, i, uses: (0, i)),
            ]
            + [pl.BlockSpec((2 * PAGE, HEAD_WIDTH), lambda h, i, uses: (0, h))] * count,
            out_specs=pl.BlockSpec((block, span), lambda h, i, uses: (i, h)),
            scratch_shapes=[
                pltpu.VMEM((count, STATE_ROWS, PAGE), jnp.bfloat16),
                pltpu.VMEM((PER_KV, STATE_ROWS, block), jnp.float32),
                pltpu.VMEM((8, block), jnp.float32),
            ],
        ),
        out_shape=jax.ShapeDtypeStruct((tokens, width), jnp.bfloat16),
        compiler_params=pltpu.CompilerParams(vmem_limit_bytes=VMEM_LIMIT),
        cost_estimate=pl.CostEstimate(
            flops=8 * tokens * PAGE * width,
            bytes_accessed=18 * 1024 * 1024,
            transcendentals=2 * tokens * PAGE * width // HEAD_WIDTH,
        ),
        name="page_attention",
    )(uses, state, adapted, page_buffer.reshape(1, tokens), *buffers)


def local(
    normed_token_input,
    queries,
    fresh_token_keys,
    fresh_token_values,
    token_request_index,
    prefix_page_cache,
    adapter_down_weight,
    adapter_up_weight,
    group_page_list,
    group_adapter_list,
    page_entry_index,
    adapter_entry_index,
):
    groups = lax.axis_size("grp")
    columns = columns_of(groups)
    rank_width = adapter_down_weight.shape[1]
    stored_pages, _, page_tokens, key_width = prefix_page_cache.shape

    onward = [(i, i + 1) for i in range(groups - 1)]
    ids_before = lax.ppermute(token_request_index + 1, "grp", onward) - 1
    keys_before = lax.ppermute(fresh_token_keys, "grp", onward)
    values_before = lax.ppermute(fresh_token_values, "grp", onward)

    adapters = jnp.concatenate([adapter_down_weight, adapter_up_weight], axis=1)
    factors, adapter_buffer_of = deliver(
        adapters, group_adapter_list, groups, columns, "pick_adapters"
    )
    pages, page_buffer_of = deliver(
        prefix_page_cache.reshape(stored_pages, 2 * page_tokens, key_width),
        group_page_list,
        groups,
        columns,
        "pick_pages",
    )

    requests = jnp.arange(page_entry_index.shape[0], dtype=jnp.int32)
    member = token_request_index[:, None] == requests[None, :]

    def by_token(entry_index, buffer_of):
        entries = jnp.arange(buffer_of.shape[0], dtype=jnp.int32)
        chosen = jnp.sum(
            jnp.where(entry_index[:, None] == entries[None, :], buffer_of[None, :], 0), axis=1
        )
        return jnp.sum(jnp.where(member, chosen[None, :], 0), axis=1)

    adapter_buffer = by_token(adapter_entry_index, adapter_buffer_of)
    page_buffer = by_token(page_entry_index, page_buffer_of)

    both_ids = jnp.concatenate([ids_before, token_request_index])
    begin = jnp.sum(
        (both_ids[None, :] < token_request_index[:, None]).astype(jnp.int32), axis=1
    )

    partial = low_rank_part(normed_token_input, factors, rank_width)
    if lax.axis_size("tp") == 2:
        total = partial + lax.ppermute(partial, "tp", [(0, 1), (1, 0)])
    else:
        total = lax.psum(partial, "tp")
    lane_buffer = jnp.arange(total.shape[1], dtype=jnp.int32) // rank_width
    low_rank = jnp.where(
        adapter_buffer[:, None] == lane_buffer[None, :], total, 0.0
    ).astype(jnp.bfloat16)

    state, adapted = fresh_attention(
        queries,
        low_rank,
        factors,
        rank_width,
        keys_before,
        values_before,
        fresh_token_keys,
        fresh_token_values,
        begin,
    )
    return page_attention(state, adapted, pages, page_buffer)


def solution(mesh):
    placed = (
        P("grp", "tp"),
        P("grp", "tp"),
        P("grp", "tp"),
        P("grp", "tp"),
        P("grp"),
        P("grp", None, None, "tp"),
        P("grp", None, "tp"),
        P("grp", None, "tp"),
        P(),
        P(),
        P(),
        P(),
    )
    return jax.shard_map(
        local, mesh=mesh, in_specs=placed, out_specs=P("grp", "tp"), check_vma=False
    )
```

time: 628 us -> 282 us (0.45); the launches traced: 621 us -> 284 us
  matrix products: 205 us -> 0 us
  waiting for transfers between devices: 210 us -> 19.9 us
  Pallas kernels: 0 us -> 150 us
  loops' own time: 81.5 us -> 0.01 us
  starting transfers between devices: 6.87 us -> 85.5 us
  local copies, waits for them, and re-layouts: 45.7 us -> 7.43 us
  other arithmetic: 54.5 us -> 19.4 us
  between operations: 13.3 us -> 1.84 us
    dot_general x69 -> x0, matrix products: 205 us -> none  [the longest x32 103 us: one_block(): jnp.dot(weights, value_head, preferred_element_type=jnp.float32)]
    pallas_call x0 -> x5, Pallas kernels: none -> 150 us  [the longest x1 81 us: fresh_attention(): pl.pallas_call(body, grid_spec=pltpu.PrefetchScalarGridSpec(num_scalar_pr...]
    all_gather x3 -> x0, waiting for transfers between devices: 146 us -> none  [the longest x1 99 us: local(): lax.all_gather(prefix_page_cache, 'grp', axis=0, tiled=True)]
    another operation x1 -> x2, loops' own time: 81.5 us -> 0.01 us  [deliver(): lax.while_loop(lambda carry: carry[0] < rounds, another, (jnp.int32(1), t...]
    ppermute x2 -> x22, starting transfers between devices: 6.79 us -> 85.5 us  [the longest x6 32.7 us: exchange(): lax.ppermute(units[m], 'grp', [(i, i ^ m) for i in range(groups)])]
    ppermute x2 -> x22, waiting for transfers between devices: 62 us -> 19.9 us  [the longest x6 16.6 us: gather_column(): upper = lax.ppermute(upper, 'grp', up)]
    reduce_sum x34 -> x10, other arithmetic: 42.8 us -> 8.82 us  [the longest x2 2.7 us: exchange(): some = jnp.sum(here, axis=1)]
    dynamic_slice x32 -> x0, local copies, waits for them, and re-layouts: 19 us -> none  [local(): lax.map(one_block, jnp.arange(heads_local * nblocks, dtype=jnp.int32))]
  transfers between devices with their start and end apart: 5 -> 22, of which waited for: 3 -> 4; matrix products, arithmetic and copies ran while one was open for 5% -> 7% of each run, Pallas kernels for 0% -> 43%
where the time goes in v1:
time: 282 us; the launch traced here: 284 us
  Pallas kernels  150 us (53%)
  starting transfers between devices  85.5 us (30%)
  waiting for transfers between devices  19.9 us (7%)
  other arithmetic  19.4 us (7%)
  local copies, waits for them, and re-layouts  7.43 us (3%)
    pallas_call x1, Pallas kernels, fresh_attention(): pl.pallas_call(body, grid_spec=pltpu.PrefetchScalarGridSpec(num_scalar_pr...  81 us
    pallas_call x2, Pallas kernels, pick_units(): pl.pallas_call(body, out_shape=[jax.ShapeDtypeStruct(unit, stacks[0].dtyp...  39.5 us
    ppermute x6, starting transfers between devices, exchange(): lax.ppermute(units[m], 'grp', [(i, i ^ m) for i in range(groups)])  32.7 us
    ppermute x6, starting transfers between devices, gather_column(): lower = lax.ppermute(lower, 'grp', down)  29.6 us
    pallas_call x1, Pallas kernels, page_attention(): pl.pallas_call(body, grid_spec=pltpu.PrefetchScalarGridSpec(num_scalar_pr...  26.5 us
    ppermute x6, waiting for transfers between devices, gather_column(): upper = lax.ppermute(upper, 'grp', up)  16.6 us
    ppermute x6, starting transfers between devices, gather_column(): upper = lax.ppermute(upper, 'grp', up)  12.8 us
    unnamed x31, local copies, waits for them, and re-layouts  6.01 us
  transfers between devices with their start and end apart: 22, of which 4 were waited for; matrix products, arithmetic and copies ran while one was open for 7% of the time, Pallas kernels for 43%

profile of v1, /device:TPU:16, one launch (start us, length us, event | category | flops | bytes accessed | tf_op | source)
XLA Modules:
  0.0 283.8 jit_solution(8148855074004863360)
XLA Ops:
  0.0 0.9 constant_dynamic-update-slice_fusion.1
  0.9 0.9 constant_dynamic-update-slice_fusion.refs_3_
  1.8 2.4 collective-permute-start.10
  4.2 3.5 %collective-permute-start.7 = (bf16[2,32,2048]{2,1,0:T(8,128)(2,1)S(1)}, bf16[2,32,2048]{2,1,0:T(8,128)(2,1)S(1)}, u32[]{:S(2)}, u32[]{:S(2)}) collective-permute-start(bf16[2,32,2048]{2,1,0:T(8,128)(2,1)S(1)} %constant_dynamic-update-slice_fusion.refs_3_), channel_id=1, source_target_pairs={{0,8},{2,10},{4,12},{6,14},{8,16},{10,18},{12,20},{14,22},{16,24},... | collective-permute-start | bytes 786440 | tf_op jit(solution)/shard_map/ppermute | solution.py:43
  7.7 2.3 collective-permute-start.22
  10.2 0.7 add_select_fusion.3
  10.9 0.7 add_select_fusion.6
  11.7 1.1 multiply_reduce_fusion.1
  13.0 0.2 reduce-window.34
  13.2 0.2 reduce-window.35
  13.3 1.3 convert_reduce_fusion.6
  14.7 1.9 collective-permute-start.11
  16.7 3.9 %collective-permute-start.8 = (bf16[2,32,2048]{2,1,0:T(8,128)(2,1)S(1)}, bf16[2,32,2048]{2,1,0:T(8,128)(2,1)}, u32[]{:S(2)}, u32[]{:S(2)}) collective-permute-start(bf16[2,32,2048]{2,1,0:T(8,128)(2,1)S(1)} %collective-permute-done.7.refs_2_), channel_id=1, source_target_pairs={{0,8},{2,10},{4,12},{6,14},{8,16},{10,18},{12,20},{14,22},{16,24},... | collective-permute-start | bytes 786440 | tf_op jit(solution)/shard_map/ppermute | solution.py:43
  20.6 0.2 select_reduce_fusion.11
  21.0 0.5 slice_bitcast_fusion
  21.5 7.1 %collective-permute-done.11.refs_5_ = bf16[2,32,2048]{2,1,0:T(8,128)(2,1)S(1)} collective-permute-done((bf16[2,32,2048]{2,1,0:T(8,128)(2,1)S(1)}, bf16[2,32,2048]{2,1,0:T(8,128)(2,1)S(1)}, u32[]{:S(2)}, u32[]{:S(2)}) %collective-permute-start.11) | collective-permute-done | bytes 262176 | tf_op jit(solution)/shard_map/ppermute | solution.py:44
  28.6 2.3 collective-permute-start.12
  31.0 4.2 %collective-permute-start.9 = (bf16[2,32,2048]{2,1,0:T(8,128)(2,1)}, bf16[2,32,2048]{2,1,0:T(8,128)(2,1)}, u32[]{:S(2)}, u32[]{:S(2)}) collective-permute-start(bf16[2,32,2048]{2,1,0:T(8,128)(2,1)} %collective-permute-done.8.refs_1_), channel_id=1, source_target_pairs={{0,8},{2,10},{4,12},{6,14},{8,16},{10,18},{12,20},{14,22},{16,24},... | collective-permute-start | bytes 786440 | tf_op jit(solution)/shard_map/ppermute | solution.py:43
  35.2 0.6 pad_add_fusion.3.wanted_ref
  35.8 0.6 reduce_max.18
  37.1 1.3 broadcast_add_fusion.1
  38.3 1.3 collective-permute-done.9.refs_0_
  39.6 5.9 %pick_adapters.2 = (bf16[32,2048]{1,0:T(8,128)(2,1)}, bf16[32,2048]{1,0:T(8,128)(2,1)}, bf16[32,2048]{1,0:T(8,128)(2,1)}, bf16[32,2048]{1,0:T(8,128)(2,1)}) custom-call(s32[4,2]{1,0:T(4,128)} %pad_add_fusion.3.wanted_ref, bf16[2,32,2048]{2,1,0:T(8,128)(2,1)} %collective-permute-done.9.refs_0_, bf16[2,32,2048]{2,1,0:T(8,128)(2,1)} %collective-permute-done.8.refs_1_, ...), custom_call_target="tpu_custom_call" | custom-call | tf_op jit(solution)/shard_map/pick_adapters/pallas_call | solution.py:70
  45.5 5.5 %collective-permute-start.13 = (bf16[32,2048]{1,0:T(8,128)(2,1)}, bf16[32,2048]{1,0:T(8,128)(2,1)S(1)}, u32[]{:S(2)}, u32[]{:S(2)}) collective-permute-start(bf16[32,2048]{1,0:T(8,128)(2,1)} %get-tuple-element.246), channel_id=1, source_target_pairs={{0,2},{2,0},{4,6},{6,4},{8,10},{10,8},{12,14},{14,12},{16,18},{18,... | collective-permute-start | bytes 393224 | tf_op jit(solution)/shard_map/ppermute | solution.py:115
  51.0 1.5 collective-permute-start.15
  52.5 0.5 bitcast_select_fusion
  53.0 8.6 %collective-permute-start.19 = (bf16[2,256,512]{2,1,0:T(8,128)(2,1)}, bf16[2,256,512]{2,1,0:T(8,128)(2,1)}, u32[]{:S(2)}, u32[]{:S(2)}) collective-permute-start(bf16[2,256,512]{2,1,0:T(8,128)(2,1)} %bitcast.68), channel_id=1, source_target_pairs={{0,8},{2,10},{4,12},{6,14},{8,16},{10,18},{12,20},{14,22},{16,24},... | collective-permute-start | bytes 1572872 | tf_op jit(solution)/shard_map/ppermute | solution.py:43
  61.6 0.6 copy-done.4
  62.3 3.5 %collective-permute-start.6 = (s32[1024]{0:T(1024)}, s32[1024]{0:T(1024)S(1)}, u32[]{:S(2)}, u32[]{:S(2)}) collective-permute-start(s32[1024]{0:T(1024)} %broadcast_add_fusion.1), channel_id=1, source_target_pairs={{0,2},{2,4},{4,6},{6,8},{8,10},{10,12},{12,14},{14,16},{16,18},{18... | collective-permute-start | bytes 12296 | tf_op jit(solution)/shard_map/ppermute | solution.py:399
  65.8 3.4 %collective-permute-start.17 = (bf16[1024,512]{1,0:T(8,128)(2,1)S(1)}, bf16[1024,512]{1,0:T(8,128)(2,1)S(1)}, u32[]{:S(2)}, u32[]{:S(2)}) collective-permute-start(bf16[1024,512]{1,0:T(8,128)(2,1)S(1)} %copy-done.2), channel_id=1, source_target_pairs={{0,2},{2,4},{4,6},{6,8},{8,10},{10,12},{12,14},{14,16},{16,18},{18... | collective-permute-start | bytes 3145736 | tf_op jit(solution)/shard_map/ppermute | solution.py:400
  69.4 0.2 reduce-window.32
  69.6 0.2 reduce-window.33
  69.8 0.2 select_reduce_fusion.13
  70.0 0.5 slice_bitcast_fusion.1
  70.5 1.4 convert_reduce_fusion.5
  71.9 0.1 copy.74
  72.0 0.1 copy.73
  72.1 0.7 select_reduce_fusion.12
  72.8 0.7 select_reduce_fusion.10
  73.6 1.4 select_reduce_fusion.4
  75.0 0.7 pad_add_fusion.4.wanted_ref
  75.6 0.1 fusion
  75.8 0.5 bitcast_select_fusion.1
  76.3 0.5 and_select_fusion
  76.8 1.3 reduce_max.19
  78.7 3.4 %collective-permute-start.18 = (bf16[1024,512]{1,0:T(8,128)(2,1)S(1)}, bf16[1024,512]{1,0:T(8,128)(2,1)}, u32[]{:S(2)}, u32[]{:S(2)}) collective-permute-start(bf16[1024,512]{1,0:T(8,128)(2,1)S(1)} %copy-done.3), channel_id=1, source_target_pairs={{0,2},{2,4},{4,6},{6,8},{8,10},{10,12},{12,14},{14,16},{16,18},{18... | collective-permute-start | bytes 3145736 | tf_op jit(solution)/shard_map/ppermute | solution.py:401
  82.1 1.9 collective-permute-start.23
  84.0 4.7 %collective-permute-start.20 = (bf16[2,256,512]{2,1,0:T(8,128)(2,1)}, bf16[2,256,512]{2,1,0:T(8,128)(2,1)}, u32[]{:S(2)}, u32[]{:S(2)}) collective-permute-start(bf16[2,256,512]{2,1,0:T(8,128)(2,1)} %collective-permute-done.19.refs_2_), channel_id=1, source_target_pairs={{0,8},{2,10},{4,12},{6,14},{8,16},{10,18},{12,20},{14,22},{16,24},... | collective-permute-start | bytes 1572872 | tf_op jit(solution)/shard_map/ppermute | solution.py:43
  88.8 0.7 pad_add_fusion.2
  89.5 1.6 convert_reduce_fusion.2
  91.2 2.2 copy-done
  93.4 2.9 %low_rank_part.1 = f32[1024,64]{1,0:T(8,128)S(1)} custom-call(bf16[1024,2048]{1,0:T(8,128)(2,1)S(1)} %copy-done, bf16[32,2048]{1,0:T(8,128)(2,1)} %get-tuple-element.249.refs_0_, bf16[32,2048]{1,0:T(8,128)(2,1)} %get-tuple-element.250.refs_1_, bf16[32,2048]{1,0:T(8,128)(2,1)} %get-tuple-element.251.refs_2_, bf16[32,2048]{1,0:T(8,128)(2,1)} %get-tuple-element.252.refs_3_), custom_call_target="tpu_custom_call" | custom-call | flops 268435456 | bytes 4194304 | tf_op jit(solution)/shard_map/low_rank_part/pallas_call | solution.py:158
  96.3 1.9 collective-permute-start.24
  98.3 4.7 %collective-permute-start.21 = (bf16[2,256,512]{2,1,0:T(8,128)(2,1)}, bf16[2,256,512]{2,1,0:T(8,128)(2,1)}, u32[]{:S(2)}, u32[]{:S(2)}) collective-permute-start(bf16[2,256,512]{2,1,0:T(8,128)(2,1)} %collective-permute-done.20.refs_1_), channel_id=1, source_target_pairs={{0,8},{2,10},{4,12},{6,14},{8,16},{10,18},{12,20},{14,22},{16,24},... | collective-permute-start | bytes 1572872 | tf_op jit(solution)/shard_map/ppermute | solution.py:43
  103.0 0.1 slice_reduce_fusion
  103.2 0.2 select_convert_fusion.lr_ref
  103.4 9.5 %collective-permute-done.24.refs_6_ = bf16[2,256,512]{2,1,0:T(8,128)(2,1)} collective-permute-done((bf16[2,256,512]{2,1,0:T(8,128)(2,1)}, bf16[2,256,512]{2,1,0:T(8,128)(2,1)}, u32[]{:S(2)}, u32[]{:S(2)}) %collective-permute-start.24) | collective-permute-done | bytes 524320 | tf_op jit(solution)/shard_map/ppermute | solution.py:44
  112.8 2.0 collective-permute-done.21.refs_0_
  114.9 33.6 %pick_pages.2 = (bf16[256,512]{1,0:T(8,128)(2,1)}, bf16[256,512]{1,0:T(8,128)(2,1)}, bf16[256,512]{1,0:T(8,128)(2,1)}, bf16[256,512]{1,0:T(8,128)(2,1)}) custom-call(s32[4,2]{1,0:T(4,128)} %pad_add_fusion.4.wanted_ref, bf16[2,256,512]{2,1,0:T(8,128)(2,1)} %collective-permute-done.21.refs_0_, bf16[2,256,512]{2,1,0:T(8,128)(2,1)} %collective-permute-done.20.refs_1_, ...), custom_call_target="tpu_custom_call" | custom-call | tf_op jit(solution)/shard_map/pick_pages/pallas_call | solution.py:70
  148.5 3.1 %collective-permute-start.25 = (bf16[256,512]{1,0:T(8,128)(2,1)}, bf16[256,512]{1,0:T(8,128)(2,1)}, u32[]{:S(2)}, u32[]{:S(2)}) collective-permute-start(bf16[256,512]{1,0:T(8,128)(2,1)} %get-tuple-element.256), channel_id=1, source_target_pairs={{0,2},{2,0},{4,6},{6,4},{8,10},{10,8},{12,14},{14,12},{16,18},{18,... | collective-permute-start | bytes 786440 | tf_op jit(solution)/shard_map/ppermute | solution.py:115
  151.5 22.6 %collective-permute-start.26 = (bf16[256,512]{1,0:T(8,128)(2,1)}, bf16[256,512]{1,0:T(8,128)(2,1)}, u32[]{:S(2)}, u32[]{:S(2)}) collective-permute-start(bf16[256,512]{1,0:T(8,128)(2,1)} %get-tuple-element.257), channel_id=1, source_target_pairs={{0,4},{2,6},{4,0},{6,2},{8,12},{10,14},{12,8},{14,10},{16,20},{18,... | collective-permute-start | bytes 786440 | tf_op jit(solution)/shard_map/ppermute | solution.py:115
  174.1 81.0 %fresh_attention.1 = (f32[16,144,1024]{2,1,0:T(8,128)}, bf16[1024,2048]{1,0:T(8,128)(2,1)}) custom-call(s32[4]{0:T(128)S(1)} %and_select_fusion.1.first_ref, bf16[1024,2048]{1,0:T(8,128)(2,1)} %q_ref.1, bf16[1024,64]{1,0:T(8,128)(2,1)S(1)} %select_convert_fusion.lr_ref, bf16[1024,512]{1,0:T(8,128)(2,1)S(1)} %collective-permute-done.17.kb_ref, ...), custom_call_target="tpu_custom_call" | custom-call | flops 4294967296 | bytes 20971520 | tf_op jit(solution)/shard_map/fresh_attention/pallas_call | solution.py:258
  255.2 2.2 copy-done.1
  257.3 26.5 %page_attention.1 = bf16[1024,2048]{1,0:T(8,128)(2,1)} custom-call(s32[4,4]{1,0:T(4,128)S(1)} %convert_element_type.89.uses_ref, f32[16,144,1024]{2,1,0:T(8,128)} %get-tuple-element.253.state_ref, bf16[1024,2048]{1,0:T(8,128)(2,1)S(1)} %copy-done.1, s32[1,1024]{1,0:T(1,128)S(1)} %bitcast.65, bf16[256,512]{1,0:T(8,128)(2,1)} %get-tuple-element.259.refs_0_, ...), custom_call_target="tpu_custom_call" | custom-call | flops 2147483648 | bytes 18874368 | tf_op jit(solution)/shard_map/page_attention/pallas_call | solution.py:350
  (80 shorter events, 0.9 us)
Async XLA Ops:
  1.8 12.9 %collective-permute-start.10 = (bf16[2,32,2048]{2,1,0:T(8,128)(2,1)S(1)}, bf16[2,32,2048]{2,1,0:T(8,128)(2,1)S(1)}, u32[]{:S(2)}, u32[]{:S(2)}) collective-permute-start(bf16[2,32,2048]{2,1,0:T(8,128)(2,1)S(1)} %constant_dynamic-update-slice_fusion.refs_3_), channel_id=1, source_target_pairs={{8,0},{10,2},{12,4},{14,6},{16,8},{18,10},{20,12},{22,14},{24,16},... | collective-permute-start | bytes 786440 | tf_op jit(solution)/shard_map/ppermute | solution.py:44
  4.2 12.4 %collective-permute-start.7 = (bf16[2,32,2048]{2,1,0:T(8,128)(2,1)S(1)}, bf16[2,32,2048]{2,1,0:T(8,128)(2,1)S(1)}, u32[]{:S(2)}, u32[]{:S(2)}) collective-permute-start(bf16[2,32,2048]{2,1,0:T(8,128)(2,1)S(1)} %constant_dynamic-update-slice_fusion.refs_3_), channel_id=1, source_target_pairs={{0,8},{2,10},{4,12},{6,14},{8,16},{10,18},{12,20},{14,22},{16,24},... | collective-permute-start | bytes 786440 | tf_op jit(solution)/shard_map/ppermute | solution.py:43
  7.7 74.4 %collective-permute-start.22 = (bf16[2,256,512]{2,1,0:T(8,128)(2,1)}, bf16[2,256,512]{2,1,0:T(8,128)(2,1)}, u32[]{:S(2)}, u32[]{:S(2)}) collective-permute-start(bf16[2,256,512]{2,1,0:T(8,128)(2,1)} %bitcast.67), channel_id=1, source_target_pairs={{8,0},{10,2},{12,4},{14,6},{16,8},{18,10},{20,12},{22,14},{24,16},... | collective-permute-start | bytes 1572872 | tf_op jit(solution)/shard_map/ppermute | solution.py:44
  11.7 3.0 %copy-start.12 = (s32[16,4]{0,1:T(4,128)}, s32[16,4]{0,1:T(4,128)S(1)}, u32[]{:S(2)}) copy-start(s32[16,4]{0,1:T(4,128)S(1)} %get-tuple-element.342) | copy-start | bytes 772
  12.8 63.0 %copy-start.8 = (s32[4,4]{1,0:T(4,128)}, s32[4,4]{1,0:T(4,128)S(1)}, u32[]{:S(2)}) copy-start(s32[4,4]{1,0:T(4,128)S(1)} %get-tuple-element.912) | copy-start | bytes 196
  12.8 63.0 %copy-start.9 = (s32[4,4]{1,0:T(4,128)}, s32[4,4]{1,0:T(4,128)S(1)}, u32[]{:S(2)}) copy-start(s32[4,4]{1,0:T(4,128)S(1)} %get-tuple-element.913) | copy-start | bytes 196
  12.9 1.8 copy-start.11
  14.7 13.9 %collective-permute-start.11 = (bf16[2,32,2048]{2,1,0:T(8,128)(2,1)S(1)}, bf16[2,32,2048]{2,1,0:T(8,128)(2,1)S(1)}, u32[]{:S(2)}, u32[]{:S(2)}) collective-permute-start(bf16[2,32,2048]{2,1,0:T(8,128)(2,1)S(1)} %collective-permute-done.10.refs_4_), channel_id=1, source_target_pairs={{8,0},{10,2},{12,4},{14,6},{16,8},{18,10},{20,12},{22,14},{24,16},... | collective-permute-start | bytes 786440 | tf_op jit(solution)/shard_map/ppermute | solution.py:44
  16.7 14.3 %collective-permute-start.8 = (bf16[2,32,2048]{2,1,0:T(8,128)(2,1)S(1)}, bf16[2,32,2048]{2,1,0:T(8,128)(2,1)}, u32[]{:S(2)}, u32[]{:S(2)}) collective-permute-start(bf16[2,32,2048]{2,1,0:T(8,128)(2,1)S(1)} %collective-permute-done.7.refs_2_), channel_id=1, source_target_pairs={{0,8},{2,10},{4,12},{6,14},{8,16},{10,18},{12,20},{14,22},{16,24},... | collective-permute-start | bytes 786440 | tf_op jit(solution)/shard_map/ppermute | solution.py:43
  28.6 9.7 %collective-permute-start.12 = (bf16[2,32,2048]{2,1,0:T(8,128)(2,1)S(1)}, bf16[2,32,2048]{2,1,0:T(8,128)(2,1)}, u32[]{:S(2)}, u32[]{:S(2)}) collective-permute-start(bf16[2,32,2048]{2,1,0:T(8,128)(2,1)S(1)} %collective-permute-done.11.refs_5_), channel_id=1, source_target_pairs={{8,0},{10,2},{12,4},{14,6},{16,8},{18,10},{20,12},{22,14},{24,16},... | collective-permute-start | bytes 786440 | tf_op jit(solution)/shard_map/ppermute | solution.py:44
  31.0 8.6 %collective-permute-start.9 = (bf16[2,32,2048]{2,1,0:T(8,128)(2,1)}, bf16[2,32,2048]{2,1,0:T(8,128)(2,1)}, u32[]{:S(2)}, u32[]{:S(2)}) collective-permute-start(bf16[2,32,2048]{2,1,0:T(8,128)(2,1)} %collective-permute-done.8.refs_1_), channel_id=1, source_target_pairs={{0,8},{2,10},{4,12},{6,14},{8,16},{10,18},{12,20},{14,22},{16,24},... | collective-permute-start | bytes 786440 | tf_op jit(solution)/shard_map/ppermute | solution.py:43
  45.5 16.1 %collective-permute-start.13 = (bf16[32,2048]{1,0:T(8,128)(2,1)}, bf16[32,2048]{1,0:T(8,128)(2,1)S(1)}, u32[]{:S(2)}, u32[]{:S(2)}) collective-permute-start(bf16[32,2048]{1,0:T(8,128)(2,1)} %get-tuple-element.246), channel_id=1, source_target_pairs={{0,2},{2,0},{4,6},{6,4},{8,10},{10,8},{12,14},{14,12},{16,18},{18,... | collective-permute-start | bytes 393224 | tf_op jit(solution)/shard_map/ppermute | solution.py:115
  51.0 10.6 %collective-permute-start.14 = (bf16[32,2048]{1,0:T(8,128)(2,1)}, bf16[32,2048]{1,0:T(8,128)(2,1)S(1)}, u32[]{:S(2)}, u32[]{:S(2)}) collective-permute-start(bf16[32,2048]{1,0:T(8,128)(2,1)} %get-tuple-element.247), channel_id=1, source_target_pairs={{0,4},{2,6},{4,0},{6,2},{8,12},{10,14},{12,8},{14,10},{16,20},{18,... | collective-permute-start | bytes 393224 | tf_op jit(solution)/shard_map/ppermute | solution.py:115
  51.0 10.6 %collective-permute-start.15 = (bf16[32,2048]{1,0:T(8,128)(2,1)}, bf16[32,2048]{1,0:T(8,128)(2,1)S(1)}, u32[]{:S(2)}, u32[]{:S(2)}) collective-permute-start(bf16[32,2048]{1,0:T(8,128)(2,1)} %get-tuple-element.248), channel_id=1, source_target_pairs={{0,6},{2,4},{4,2},{6,0},{8,14},{10,12},{12,10},{14,8},{16,22},{18,... | collective-permute-start | bytes 393224 | tf_op jit(solution)/shard_map/ppermute | solution.py:115
  53.0 31.0 %collective-permute-start.19 = (bf16[2,256,512]{2,1,0:T(8,128)(2,1)}, bf16[2,256,512]{2,1,0:T(8,128)(2,1)}, u32[]{:S(2)}, u32[]{:S(2)}) collective-permute-start(bf16[2,256,512]{2,1,0:T(8,128)(2,1)} %bitcast.68), channel_id=1, source_target_pairs={{0,8},{2,10},{4,12},{6,14},{8,16},{10,18},{12,20},{14,22},{16,24},... | collective-permute-start | bytes 1572872 | tf_op jit(solution)/shard_map/ppermute | solution.py:43
  61.6 0.7 copy-start.4
  61.6 0.7 copy-start.6
  61.6 0.7 copy-start.7
  62.3 3.5 %copy-start.2 = (bf16[1024,512]{1,0:T(8,128)(2,1)S(1)}, bf16[1024,512]{1,0:T(8,128)(2,1)}, u32[]{:S(2)}) copy-start(bf16[1024,512]{1,0:T(8,128)(2,1)} %k_ref.1) | copy-start | bytes 3145732
  62.3 16.4 %copy-start.3 = (bf16[1024,512]{1,0:T(8,128)(2,1)S(1)}, bf16[1024,512]{1,0:T(8,128)(2,1)}, u32[]{:S(2)}) copy-start(bf16[1024,512]{1,0:T(8,128)(2,1)} %v_ref.1) | copy-start | bytes 3145732
  62.3 26.4 %collective-permute-start.6 = (s32[1024]{0:T(1024)}, s32[1024]{0:T(1024)S(1)}, u32[]{:S(2)}, u32[]{:S(2)}) collective-permute-start(s32[1024]{0:T(1024)} %broadcast_add_fusion.1), channel_id=1, source_target_pairs={{0,2},{2,4},{4,6},{6,8},{8,10},{10,12},{12,14},{14,16},{16,18},{18... | collective-permute-start | bytes 12296 | tf_op jit(solution)/shard_map/ppermute | solution.py:399
  65.8 108.3 %collective-permute-start.17 = (bf16[1024,512]{1,0:T(8,128)(2,1)S(1)}, bf16[1024,512]{1,0:T(8,128)(2,1)S(1)}, u32[]{:S(2)}, u32[]{:S(2)}) collective-permute-start(bf16[1024,512]{1,0:T(8,128)(2,1)S(1)} %copy-done.2), channel_id=1, source_target_pairs={{0,2},{2,4},{4,6},{6,8},{8,10},{10,12},{12,14},{14,16},{16,18},{18... | collective-permute-start | bytes 3145736 | tf_op jit(solution)/shard_map/ppermute | solution.py:400
  69.3 3.6 %copy-start.10 = (s32[4]{0:T(128)}, s32[4]{0:T(128)S(1)}, u32[]{:S(2)}) copy-start(s32[4]{0:T(128)S(1)} %fusion.16) | copy-start | bytes 52
  78.7 95.4 %collective-permute-start.18 = (bf16[1024,512]{1,0:T(8,128)(2,1)S(1)}, bf16[1024,512]{1,0:T(8,128)(2,1)}, u32[]{:S(2)}, u32[]{:S(2)}) collective-permute-start(bf16[1024,512]{1,0:T(8,128)(2,1)S(1)} %copy-done.3), channel_id=1, source_target_pairs={{0,2},{2,4},{4,6},{6,8},{8,10},{10,12},{12,14},{14,16},{16,18},{18... | collective-permute-start | bytes 3145736 | tf_op jit(solution)/shard_map/ppermute | solution.py:401
  82.1 14.2 %collective-permute-start.23 = (bf16[2,256,512]{2,1,0:T(8,128)(2,1)}, bf16[2,256,512]{2,1,0:T(8,128)(2,1)}, u32[]{:S(2)}, u32[]{:S(2)}) collective-permute-start(bf16[2,256,512]{2,1,0:T(8,128)(2,1)} %collective-permute-done.22.refs_4_), channel_id=1, source_target_pairs={{8,0},{10,2},{12,4},{14,6},{16,8},{18,10},{20,12},{22,14},{24,16},... | collective-permute-start | bytes 1572872 | tf_op jit(solution)/shard_map/ppermute | solution.py:44
  84.0 14.2 %collective-permute-start.20 = (bf16[2,256,512]{2,1,0:T(8,128)(2,1)}, bf16[2,256,512]{2,1,0:T(8,128)(2,1)}, u32[]{:S(2)}, u32[]{:S(2)}) collective-permute-start(bf16[2,256,512]{2,1,0:T(8,128)(2,1)} %collective-permute-done.19.refs_2_), channel_id=1, source_target_pairs={{0,8},{2,10},{4,12},{6,14},{8,16},{10,18},{12,20},{14,22},{16,24},... | collective-permute-start | bytes 1572872 | tf_op jit(solution)/shard_map/ppermute | solution.py:43
  91.1 12.0 %copy-start.13 = (s32[1024]{0:T(1024)S(1)}, s32[1024]{0:T(1024)}, u32[]{:S(2)}) copy-start(s32[1024]{0:T(1024)} %get-tuple-element.325) | copy-start | bytes 12292
  91.2 12.0 %copy-start.14 = (s32[64]{0:T(128)S(1)}, s32[64]{0:T(128)}, u32[]{:S(2)}) copy-start(s32[64]{0:T(128)} %and_select_fusion) | copy-start | bytes 772
  91.2 2.2 copy-start
  93.4 80.7 %copy-start.5 = (bf16[32,2048]{1,0:T(8,128)(2,1)S(1)}, bf16[32,2048]{1,0:T(8,128)(2,1)}, u32[]{:S(2)}) copy-start(bf16[32,2048]{1,0:T(8,128)(2,1)} %get-tuple-element.250.refs_1_) | copy-start | bytes 393220
  96.2 6.9 %collective-permute-start.16 = (f32[1024,64]{1,0:T(8,128)S(1)}, f32[1024,64]{1,0:T(8,128)S(1)}, u32[]{:S(2)}, u32[]{:S(2)}) collective-permute-start(f32[1024,64]{1,0:T(8,128)S(1)} %low_rank_part.1), channel_id=1, source_target_pairs={{0,1},{1,0},{2,3},{3,2},{4,5},{5,4},{6,7},{7,6},{8,9},{9,8},{10,11... | collective-permute-start | bytes 786440 | tf_op jit(solution)/shard_map/ppermute | solution.py:435
  96.3 16.5 %collective-permute-start.24 = (bf16[2,256,512]{2,1,0:T(8,128)(2,1)}, bf16[2,256,512]{2,1,0:T(8,128)(2,1)}, u32[]{:S(2)}, u32[]{:S(2)}) collective-permute-start(bf16[2,256,512]{2,1,0:T(8,128)(2,1)} %collective-permute-done.23.refs_5_), channel_id=1, source_target_pairs={{8,0},{10,2},{12,4},{14,6},{16,8},{18,10},{20,12},{22,14},{24,16},... | collective-permute-start | bytes 1572872 | tf_op jit(solution)/shard_map/ppermute | solution.py:44
  98.3 16.6 %collective-permute-start.21 = (bf16[2,256,512]{2,1,0:T(8,128)(2,1)}, bf16[2,256,512]{2,1,0:T(8,128)(2,1)}, u32[]{:S(2)}, u32[]{:S(2)}) collective-permute-start(bf16[2,256,512]{2,1,0:T(8,128)(2,1)} %collective-permute-done.20.refs_1_), channel_id=1, source_target_pairs={{0,8},{2,10},{4,12},{6,14},{8,16},{10,18},{12,20},{14,22},{16,24},... | collective-permute-start | bytes 1572872 | tf_op jit(solution)/shard_map/ppermute | solution.py:43
  148.5 106.6 %collective-permute-start.25 = (bf16[256,512]{1,0:T(8,128)(2,1)}, bf16[256,512]{1,0:T(8,128)(2,1)}, u32[]{:S(2)}, u32[]{:S(2)}) collective-permute-start(bf16[256,512]{1,0:T(8,128)(2,1)} %get-tuple-element.256), channel_id=1, source_target_pairs={{0,2},{2,0},{4,6},{6,4},{8,10},{10,8},{12,14},{14,12},{16,18},{18,... | collective-permute-start | bytes 786440 | tf_op jit(solution)/shard_map/ppermute | solution.py:115
  151.5 103.6 %collective-permute-start.26 = (bf16[256,512]{1,0:T(8,128)(2,1)}, bf16[256,512]{1,0:T(8,128)(2,1)}, u32[]{:S(2)}, u32[]{:S(2)}) collective-permute-start(bf16[256,512]{1,0:T(8,128)(2,1)} %get-tuple-element.257), channel_id=1, source_target_pairs={{0,4},{2,6},{4,0},{6,2},{8,12},{10,14},{12,8},{14,10},{16,20},{18,... | collective-permute-start | bytes 786440 | tf_op jit(solution)/shard_map/ppermute | solution.py:115
  174.1 81.0 %collective-permute-start.27 = (bf16[256,512]{1,0:T(8,128)(2,1)}, bf16[256,512]{1,0:T(8,128)(2,1)}, u32[]{:S(2)}, u32[]{:S(2)}) collective-permute-start(bf16[256,512]{1,0:T(8,128)(2,1)} %get-tuple-element.258), channel_id=1, source_target_pairs={{0,6},{2,4},{4,2},{6,0},{8,14},{10,12},{12,10},{14,8},{16,22},{18,... | collective-permute-start | bytes 786440 | tf_op jit(solution)/shard_map/ppermute | solution.py:115
  255.2 2.2 copy-start.1
